TPU v7x, 256 devices: a whole 4x4x8 slice. The times are simulated.
256 devices in a mesh: region: 64 (over z, y, core), sub: 4 (over x).
Axes of the slice: x: 4, y: 4, z: 8, core: 2. Of those that a mesh axis runs over, the one named last changes fastest.
Arguments:
- innovations: float32 [4096, 16, 128], P(('region', 'sub'))
- ensemble: float32 [4096, 64, 128], P(('region', 'sub')), may hold values from -3 to 3
- coords: int32 [4096, 2, 128], P(('region', 'sub')), may hold values from 0 to 255, as said below
- obs_error: float32 [4096, 128], P(('region', 'sub')), may hold values from 2.5 to 5
- pair_cols: int32 [4096, 9], P(('region', 'sub')), may hold values from 0 to 4095, as said below
- pair_count: int32 [4096], P(('region', 'sub')), may hold values from 1 to 9, as said below
Outputs:
- analysis_weights: float32 [4096, 16, 128], P(('region', 'sub'))
- residual: float32 [4096, 16, 128], P(('region', 'sub'))
Inputs may be any that keep to these rules, and one draw needn't show every extreme that they name: `coords`: the first coordinate lies in 0 to 63, the second in 0 to 255. `pair_cols`: the first pair_count[b] entries of row b list, in ascending order, the blocks paired with block b: always b itself, and only blocks c with |c - b| <= 4; c lists b exactly when b lists c. The remaining slots hold b. `pair_count`: the largest value 9 is taken in every draw.
All inputs are finite; a program needn't handle non-finite values.
Results may differ from a plain program's by a relative error of at most 0.00045.
Values sent between devices are 32-bit elements; how exact they have to be, the bound alone decides.
A program may use at most 64 MiB of HBM per device.

v0:
```python
import functools

import jax
import jax.numpy as jnp
import numpy as np
from jax import lax
from jax.experimental import pallas as pl
from jax.experimental.pallas import tpu as pltpu
from jax.sharding import PartitionSpec as P

MESH = pl.DeviceIdType.MESH
F32 = jnp.float32
BF16 = jnp.bfloat16

NB = 16
W = 4
NX = NB + 2 * W
SLOTS = 2 * W + 1
OBS = 128
RHS = 16
MEM = 64
SPAN = SLOTS * OBS

STATIC_VAR = 0.002
LOG2E = 1.4426950408889634
C_CORR = -LOG2E / 150.0
C_LOC = -LOG2E / (2.0 * 200.0**2)
ENS_SCALE = 1.0 / ((MEM - 1) * STATIC_VAR)


def split(value):
    hi = value.astype(BF16)
    lo = (value - hi.astype(F32)).astype(BF16)
    return hi, lo


def rows_of(rows, dtype=F32):
    ids = lax.broadcasted_iota(jnp.int32, (16, OBS), 0)
    out = jnp.zeros((16, OBS), F32)
    for place, row in enumerate(rows):
        out = jnp.where(ids == place, jnp.broadcast_to(row, (16, OBS)), out)
    return out.astype(dtype)


def features(crd, place):
    x = crd[0:1, :].astype(F32)
    y = crd[1:2, :].astype(F32)
    base = (place - NX // 2).astype(F32) * 64.0
    base = jnp.full((1, OBS), base, F32)
    full = x + base
    square = full * full + y * y
    s1 = square.astype(BF16).astype(F32)
    s2 = (square - s1).astype(BF16).astype(F32)
    s3 = square - s1 - s2
    one = jnp.ones((1, OBS), F32)
    left = [s1, s2, s3, one, one, one, base, base, x, x, y]
    right = [one, one, one, s1, s2, s3, -2.0 * base, -2.0 * x, -2.0 * base, -2.0 * x, -2.0 * y]
    return left, right


def kernel(
    innov, ens, coords, obs, cols, w_out, r_out,
    lhsx, rhs, kmat, zx, zf, maskx,
    ens_lo, ens_hi, crd_lo, crd_hi, v_lo, v_hi, p_lo, p_hi,
    part_a, part_b, red_a, red_b,
    halo_send, halo_recv, send_a, recv_a, send_b, recv_b,
):
    me = lax.axis_index("region") * 4 + lax.axis_index("sub")

    def device(index):
        return (lax.div(index, 4), lax.rem(index, 4))

    left = device(lax.rem(me + 255, 256))
    right = device(lax.rem(me + 1, 256))
    x = lax.rem(me, 4)
    core = lax.rem(lax.div(me, 4), 2)
    y = lax.rem(lax.div(me, 8), 4)
    z = lax.div(me, 32)

    def peer_a(step):
        there = lax.rem(y * 4 + x + step, 16)
        return device(((z * 4 + lax.div(there, 4)) * 2 + core) * 4 + lax.rem(there, 4))

    def peer_b(step):
        there = lax.rem(z * 2 + core + step, 16)
        return device(((lax.div(there, 2) * 4 + y) * 2 + lax.rem(there, 2)) * 4 + x)

    barrier = pltpu.get_barrier_semaphore()
    for there in (left, right):
        pl.semaphore_signal(barrier, inc=1, device_id=there, device_id_type=MESH)

    def greet(step, carry):
        pl.semaphore_signal(barrier, inc=1, device_id=peer_a(step), device_id_type=MESH)
        pl.semaphore_signal(barrier, inc=1, device_id=peer_b(step), device_id_type=MESH)
        return carry

    lax.fori_loop(1, 16, greet, 0)
    pl.semaphore_wait(barrier, 32)

    def remote(src, dst, slot, there):
        return pltpu.make_async_remote_copy(
            src_ref=src, dst_ref=dst, send_sem=halo_send.at[slot], recv_sem=halo_recv.at[slot],
            device_id=there, device_id_type=MESH,
        )

    static = [
        remote(ens.at[NB - W : NB], ens_lo, 0, right),
        remote(ens.at[0:W], ens_hi, 1, left),
        remote(coords.at[NB - W : NB], crd_lo, 2, right),
        remote(coords.at[0:W], crd_hi, 3, left),
        remote(innov.at[NB - W : NB], v_lo, 4, right),
        remote(innov.at[0:W], v_hi, 5, left),
    ]
    for copy in static:
        copy.start()

    own = lax.broadcasted_iota(jnp.int32, (NB, SLOTS), 0) + me * NB
    offset = cols[...] - own
    for slot in range(SLOTS):
        hit = jnp.max(jnp.where(offset == slot - W, 1.0, 0.0).astype(F32), axis=1, keepdims=True)
        wide = jnp.broadcast_to(hit, (NB, OBS))
        for b in range(NB):
            maskx[b, :, slot * OBS : (slot + 1) * OBS] = jnp.broadcast_to(wide[b : b + 1, :], (RHS, OBS)).astype(BF16)

    def lanes(place):
        return pl.ds(pl.multiple_of(place * OBS, OBS), OBS)

    def prepare(place, members, crd, vectors):
        hi, lo = split(members)
        feats, weights = features(crd, place)
        stacked = jnp.concatenate(
            [hi, hi, lo, rows_of(feats, BF16), jnp.zeros((48, OBS), BF16)], axis=0
        )
        lhsx[place] = stacked.T
        v_hi_part, v_lo_part = split(vectors)
        zx[0:16, lanes(place)] = v_hi_part
        zx[16:32, lanes(place)] = v_lo_part
        return weights

    def prepare_own(b, carry):
        members = ens[b]
        vectors = innov[b]
        weights = prepare(b + W, members, coords[b], vectors)
        hi, lo = split(members * ENS_SCALE)
        none = jnp.zeros((64, OBS), BF16)
        rhs[b, 0:64, 0:128] = hi
        rhs[b, 64:128, 0:128] = lo
        rhs[b, 128:192, 0:128] = hi
        rhs[b, 192:256, 0:128] = none
        rhs[b, 0:192, 128:256] = jnp.zeros((192, OBS), BF16)
        rhs[b, 192:208, 128:256] = rows_of(weights, BF16)
        rhs[b, 208:256, 128:256] = jnp.zeros((48, OBS), BF16)
        zf[0:16, lanes(b)] = vectors
        return carry

    lax.fori_loop(0, NB, prepare_own, 0)

    def tiles(b):
        weights = rhs[b]
        for slot in range(SLOTS):
            both = jnp.dot(lhsx[b + slot], weights, preferred_element_type=F32)
            shared = both[:, 0:128]
            square = both[:, 128:256]
            inverse = lax.rsqrt(jnp.maximum(square, 1e-30))
            value = jnp.exp2(square * C_CORR * inverse) + jnp.exp2(square * C_LOC) * shared
            hi, lo = split(value)
            kmat[b, slot * OBS : (slot + 1) * OBS, 0:128] = hi
            kmat[b, slot * OBS : (slot + 1) * OBS, 128:256] = lo

    def apply(b, row, out_row, vec):
        window = pl.ds(pl.multiple_of(b * OBS, OBS), SPAN)
        mask = maskx[b]
        vectors = jnp.concatenate([zx[row : row + 16, window] * mask, zx[row + 16 : row + 32, window] * mask], axis=0)
        part = jnp.dot(vectors, kmat[b], preferred_element_type=F32)
        part = part[0:16] + part[16:32]
        total = (part[:, 0:128] + part[:, 128:256]) * STATIC_VAR + obs[pl.ds(b, 1), :] * vec
        zf[out_row : out_row + 16, lanes(b)] = total
        hi, lo = split(total)
        zx[row + 32 : row + 48, lanes(b + W)] = hi
        zx[row + 48 : row + 64, lanes(b + W)] = lo

    def first(b, carry):
        tiles(b)
        apply(b, 0, 16, zf[0:16, lanes(b)])
        return carry

    def second(b, carry):
        apply(b, 32, 32, zf[16:32, lanes(b)])
        return carry

    lax.fori_loop(W, NB - W, first, 0)
    for copy in static:
        copy.wait()

    def prepare_halo(i, carry):
        prepare(i, ens_lo[i], crd_lo[i], v_lo[i])
        prepare(i + NB + W, ens_hi[i], crd_hi[i], v_hi[i])
        return carry

    lax.fori_loop(0, W, prepare_halo, 0)
    lax.fori_loop(0, W, first, 0)
    lax.fori_loop(NB - W, NB, first, 0)

    moving = [
        remote(zf.at[16:32, (NB - W) * OBS : NB * OBS], p_lo, 6, right),
        remote(zf.at[16:32, 0 : W * OBS], p_hi, 7, left),
    ]
    for copy in moving:
        copy.start()
    lax.fori_loop(W, NB - W, second, 0)
    for copy in moving:
        copy.wait()
    for source, start in ((p_lo, 0), (p_hi, (NB + W) * OBS)):
        hi, lo = split(source[...])
        zx[32:48, start : start + W * OBS] = hi
        zx[48:64, start : start + W * OBS] = lo
    lax.fori_loop(0, W, second, 0)
    lax.fori_loop(NB - W, NB, second, 0)

    inner = slice(W * OBS, (W + NB) * OBS)
    gram = lax.dot_general(
        zx[0:64, inner], zx[0:96, inner], (((1,), (1,)), ((), ())), preferred_element_type=F32
    )
    gram = jnp.concatenate([gram, jnp.zeros((64, 32), F32)], axis=1)
    lane = lax.broadcasted_iota(jnp.int32, (16, OBS), 1)
    lane8 = lax.broadcasted_iota(jnp.int32, (8, OBS), 1)

    def turn(value, by):
        return pltpu.roll(value, by % OBS, 1)

    of_r = gram[0:16] + gram[16:32]
    of_p = gram[32:48] + gram[48:64]
    of_r = of_r + turn(of_r, -16)
    of_p = of_p + turn(of_p, -16)
    even = (lane & 16) == 0
    own_part = jnp.where(even, of_r, turn(of_p, -16))
    part_a[...] = jnp.where(lane8 < 64, own_part[0:8], turn(own_part[8:16], 64))

    def exchange(part, red, peer, send, recv):
        def copy(step):
            return pltpu.make_async_remote_copy(
                src_ref=part, dst_ref=red.at[step - 1], send_sem=send.at[step - 1], recv_sem=recv.at[step - 1],
                device_id=peer(step), device_id_type=MESH,
            )

        def start(step, carry):
            copy(step).start()
            return carry

        def wait(step, carry):
            copy(step).wait()
            return carry

        lax.fori_loop(1, 16, start, 0)
        lax.fori_loop(1, 16, wait, 0)
        return part[...] + jnp.sum(red[...], axis=0)

    part_b[...] = exchange(part_a, red_a, peer_a, send_a, recv_a)
    packed = exchange(part_b, red_b, peer_b, send_b, recv_b)

    moments = jnp.concatenate([packed, turn(packed, 64)], axis=0)
    top = jnp.where(lane < 16, turn(moments, -32), jnp.where(lane < 32, moments, turn(moments, 32)))
    low = jnp.where(lane < 16, turn(moments, -16), jnp.where(lane < 32, turn(moments, -32), moments))
    system = jnp.concatenate([top, low], axis=0)
    rows = lax.broadcasted_iota(jnp.int32, (32, OBS), 0)
    for k in range(32):
        pivot = 1.0 / system[k : k + 1, k : k + 1]
        row = system[k : k + 1, :] * pivot
        system = jnp.where(rows == k, row, system - system[:, k : k + 1] * row)

    solved = jnp.concatenate([system, jnp.zeros((96, OBS), F32)], axis=0).T
    coeffs = solved[32:48, :]
    zero = jnp.zeros((16, OBS), F32)
    for_w = jnp.where(lane < 32, coeffs, zero)
    for_r = turn(for_w, 16)
    both = jnp.concatenate([for_w, for_r], axis=0)[:, 0:48]
    for chunk in range(4):
        out = jnp.dot(
            both, zf[:, chunk * 512 : (chunk + 1) * 512], preferred_element_type=F32, precision=lax.Precision.HIGHEST
        )
        for piece in range(4):
            b = chunk * 4 + piece
            here = out[:, piece * OBS : (piece + 1) * OBS]
            w_out[b] = here[0:16]
            r_out[b] = innov[b] - here[16:32]


def on_device(innovations, ensemble, coords, obs_error, pair_cols, pair_count):
    del pair_count
    vmem = pl.BlockSpec(memory_space=pltpu.VMEM)
    out = jax.ShapeDtypeStruct((NB, RHS, OBS), F32)
    return pl.pallas_call(
        kernel,
        out_shape=(out, out),
        in_specs=[vmem] * 5,
        out_specs=(vmem, vmem),
        scratch_shapes=[
            pltpu.VMEM((NX, OBS, 256), BF16),
            pltpu.VMEM((NB, 256, 256), BF16),
            pltpu.VMEM((NB, SPAN, 256), BF16),
            pltpu.VMEM((96, NX * OBS), BF16),
            pltpu.VMEM((48, NB * OBS), F32),
            pltpu.VMEM((NB, RHS, SPAN), BF16),
            pltpu.VMEM((W, MEM, OBS), F32),
            pltpu.VMEM((W, MEM, OBS), F32),
            pltpu.VMEM((W, 2, OBS), jnp.int32),
            pltpu.VMEM((W, 2, OBS), jnp.int32),
            pltpu.VMEM((W, RHS, OBS), F32),
            pltpu.VMEM((W, RHS, OBS), F32),
            pltpu.VMEM((RHS, W * OBS), F32),
            pltpu.VMEM((RHS, W * OBS), F32),
            pltpu.VMEM((8, OBS), F32),
            pltpu.VMEM((8, OBS), F32),
            pltpu.VMEM((15, 8, OBS), F32),
            pltpu.VMEM((15, 8, OBS), F32),
            pltpu.SemaphoreType.DMA((8,)),
            pltpu.SemaphoreType.DMA((8,)),
            pltpu.SemaphoreType.DMA((15,)),
            pltpu.SemaphoreType.DMA((15,)),
            pltpu.SemaphoreType.DMA((15,)),
            pltpu.SemaphoreType.DMA((15,)),
        ],
        compiler_params=pltpu.CompilerParams(
            collective_id=0, has_side_effects=True, vmem_limit_bytes=48 * 1024 * 1024
        ),
    )(innovations, ensemble, coords, obs_error, pair_cols)


def solution(mesh):
    both = ("region", "sub")
    in_specs = (
        P(both, None, None),
        P(both, None, None),
        P(both, None, None),
        P(both, None),
        P(both, None),
        P(both),
    )
    out_specs = (P(both, None, None), P(both, None, None))
    return jax.shard_map(on_device, mesh=mesh, in_specs=in_specs, out_specs=out_specs, check_vma=False)
```

profile of v0, /device:TPU:1, one launch (start us, length us, event | category | flops | bytes accessed | tf_op | source)
XLA Modules:
  0.0 48.3 jit_solution(18167459814443060767)
XLA Ops:
  0.6 0.0 copy-start
  0.6 1.0 %copy-done = f32[16,64,128]{2,1,0:T(8,128)S(1)} copy-done((f32[16,64,128]{2,1,0:T(8,128)S(1)}, f32[16,64,128]{2,1,0:T(8,128)}, u32[]{:S(2)}) %copy-start) | copy-done | bytes 524312
  1.7 0.0 copy-start.1
  1.7 0.9 %copy-done.1 = f32[16,16,128]{2,1,0:T(8,128)S(1)} copy-done((f32[16,16,128]{2,1,0:T(8,128)S(1)}, f32[16,16,128]{2,1,0:T(8,128)}, u32[]{:S(2)}) %copy-start.1) | copy-done | bytes 131096
  2.6 0.0 copy-start.2
  2.6 0.7 %copy-done.2 = s32[16,2,128]{2,1,0:T(2,128)S(1)} copy-done((s32[16,2,128]{2,1,0:T(2,128)S(1)}, s32[16,2,128]{2,1,0:T(2,128)}, u32[]{:S(2)}) %copy-start.2) | copy-done | bytes 16408
  3.3 0.0 copy-start.3
  3.3 0.7 %copy-done.3 = f32[16,128]{1,0:T(8,128)S(1)} copy-done((f32[16,128]{1,0:T(8,128)S(1)}, f32[16,128]{1,0:T(8,128)}, u32[]{:S(2)}) %copy-start.3) | copy-done | bytes 8216
  4.0 0.0 copy-start.4
  4.0 0.7 %copy-done.4 = s32[16,9]{1,0:T(8,128)S(1)} copy-done((s32[16,9]{1,0:T(8,128)S(1)}, s32[16,9]{1,0:T(8,128)}, u32[]{:S(2)}) %copy-start.4) | copy-done | bytes 600
  4.7 42.3 %shard_map.68 = (f32[16,16,128]{2,1,0:T(8,128)S(1)}, f32[16,16,128]{2,1,0:T(8,128)S(1)}) custom-call(f32[16,16,128]{2,1,0:T(8,128)S(1)} %copy-done.1, f32[16,64,128]{2,1,0:T(8,128)S(1)} %copy-done, s32[16,2,128]{2,1,0:T(2,128)S(1)} %copy-done.2, f32[16,128]{1,0:T(8,128)S(1)} %copy-done.3, s32[16,9]{1,0:T(8,128)S(1)} %copy-done.4), custom_call_target="tpu_custom_call" | custom-call | tf_op jit(solution)/shard_map/pallas_call | solution.py:292
  47.0 0.7 %copy.9 = f32[16,16,128]{2,1,0:T(8,128)} copy(f32[16,16,128]{2,1,0:T(8,128)S(1)} %get-tuple-element.4) | data formatting | bytes 262144
  47.6 0.7 %copy.10 = f32[16,16,128]{2,1,0:T(8,128)} copy(f32[16,16,128]{2,1,0:T(8,128)S(1)} %get-tuple-element.5) | data formatting | bytes 262144
Async XLA Ops:
  0.6 1.0 %copy-start = (f32[16,64,128]{2,1,0:T(8,128)S(1)}, f32[16,64,128]{2,1,0:T(8,128)}, u32[]{:S(2)}) copy-start(f32[16,64,128]{2,1,0:T(8,128)} %ens.1) | copy-start | bytes 1572868
  1.7 0.9 %copy-start.1 = (f32[16,16,128]{2,1,0:T(8,128)S(1)}, f32[16,16,128]{2,1,0:T(8,128)}, u32[]{:S(2)}) copy-start(f32[16,16,128]{2,1,0:T(8,128)} %innov.1) | copy-start | bytes 393220
  2.6 0.7 %copy-start.2 = (s32[16,2,128]{2,1,0:T(2,128)S(1)}, s32[16,2,128]{2,1,0:T(2,128)}, u32[]{:S(2)}) copy-start(s32[16,2,128]{2,1,0:T(2,128)} %coords.1) | copy-start | bytes 49156
  3.3 0.7 %copy-start.3 = (f32[16,128]{1,0:T(8,128)S(1)}, f32[16,128]{1,0:T(8,128)}, u32[]{:S(2)}) copy-start(f32[16,128]{1,0:T(8,128)} %obs.1) | copy-start | bytes 24580
  4.0 0.7 %copy-start.4 = (s32[16,9]{1,0:T(8,128)S(1)}, s32[16,9]{1,0:T(8,128)}, u32[]{:S(2)}) copy-start(s32[16,9]{1,0:T(8,128)} %cols.1) | copy-start | bytes 1732
where the time goes:
time: 48.6 us; the launch traced here: 48.3 us
  Pallas kernels  42.3 us (87%)
  local copies, waits for them, and re-layouts  5.36 us (11%)
  between operations  0.65 us (1%)
    pallas_call x1, Pallas kernels, on_device(): pl.pallas_call(kernel, out_shape=(out, out), in_specs=[vmem] * 5, out_spe...  42.3 us
    unnamed x12, local copies, waits for them, and re-layouts  5.36 us

commit v1 on v0

v1 whole, which is shorter than its diff:
```python
import jax
import jax.numpy as jnp
from jax import lax
from jax.experimental import pallas as pl
from jax.experimental.pallas import tpu as pltpu
from jax.sharding import PartitionSpec as P

MESH = pl.DeviceIdType.MESH
F32 = jnp.float32
BF16 = jnp.bfloat16

NB = 16
W = 4
NX = NB + 2 * W
SLOTS = 2 * W + 1
HALF = W + 1
OBS = 128
RHS = 16
MEM = 64

STATIC_VAR = 0.002
LOG2E = 1.4426950408889634
C_CORR = -LOG2E / 150.0
C_LOC = -LOG2E / (2.0 * 200.0**2)
ENS_SCALE = 1.0 / ((MEM - 1) * STATIC_VAR)


def split(value):
    hi = value.astype(BF16)
    lo = (value - hi.astype(F32)).astype(BF16)
    return hi, lo


def rows_of(rows):
    ids = lax.broadcasted_iota(jnp.int32, (16, OBS), 0)
    out = jnp.zeros((16, OBS), F32)
    for place, row in enumerate(rows):
        out = jnp.where(ids == place, jnp.broadcast_to(row, (16, OBS)), out)
    return out.astype(BF16)


def position_parts(crd, place):
    x = crd[0:1, :].astype(F32)
    y = crd[1:2, :].astype(F32)
    base = jnp.full((1, OBS), jnp.asarray(place - NX // 2).astype(F32) * 64.0, F32)
    full = x + base
    square = full * full + y * y
    s1 = square.astype(BF16).astype(F32)
    s2 = (square - s1).astype(BF16).astype(F32)
    s3 = square - s1 - s2
    return s1, s2, s3, base, x, y


def kernel(
    innov, ens, coords, obs, cols, out,
    ens_v, crd_v, v_v, obs_v, cols_v,
    lhsx, rhs, kmat, zx, zf, maskx,
    ens_lo, ens_hi, crd_lo, crd_hi, v_lo, v_hi, p_lo, p_hi,
    part_a, part_b, red_a, red_b,
    load_sem, halo_send, halo_recv, send_a, recv_a, send_b, recv_b,
):
    me = lax.axis_index("region") * 4 + lax.axis_index("sub")

    def device(index):
        return (lax.div(index, 4), lax.rem(index, 4))

    left = device(lax.rem(me + 255, 256))
    right = device(lax.rem(me + 1, 256))
    x = lax.rem(me, 4)
    core = lax.rem(lax.div(me, 4), 2)
    y = lax.rem(lax.div(me, 8), 4)
    z = lax.div(me, 32)

    def peer_a(step):
        there = lax.rem(y * 4 + x + step, 16)
        return device(((z * 4 + lax.div(there, 4)) * 2 + core) * 4 + lax.rem(there, 4))

    def peer_b(step):
        there = lax.rem(z * 2 + core + step, 16)
        return device(((lax.div(there, 2) * 4 + y) * 2 + lax.rem(there, 2)) * 4 + x)

    barrier = pltpu.get_barrier_semaphore()
    for there in (left, right):
        pl.semaphore_signal(barrier, inc=1, device_id=there, device_id_type=MESH)

    def greet(step, carry):
        pl.semaphore_signal(barrier, inc=1, device_id=peer_a(step), device_id_type=MESH)
        pl.semaphore_signal(barrier, inc=1, device_id=peer_b(step), device_id_type=MESH)
        return carry

    lax.fori_loop(1, 16, greet, 0)
    loads = [
        pltpu.make_async_copy(source, target, load_sem.at[i])
        for i, (source, target) in enumerate(
            ((cols, cols_v), (coords, crd_v), (ens, ens_v), (innov, v_v), (obs, obs_v))
        )
    ]
    for load in loads:
        load.start()
    pl.semaphore_wait(barrier, 32)

    def remote(src, dst, slot, there):
        return pltpu.make_async_remote_copy(
            src_ref=src, dst_ref=dst, send_sem=halo_send.at[slot], recv_sem=halo_recv.at[slot],
            device_id=there, device_id_type=MESH,
        )

    static = [
        remote(ens.at[NB - W : NB], ens_lo, 0, right),
        remote(ens.at[0:W], ens_hi, 1, left),
        remote(coords.at[NB - W : NB], crd_lo, 2, right),
        remote(coords.at[0:W], crd_hi, 3, left),
        remote(innov.at[NB - W : NB], v_lo, 4, right),
        remote(innov.at[0:W], v_hi, 5, left),
    ]
    for copy in static:
        copy.start()
    for load in loads:
        load.wait()

    offset = cols_v[...] - (lax.broadcasted_iota(jnp.int32, (NB, SLOTS), 0) + me * NB)
    for slot in range(SLOTS):
        hit = jnp.max(jnp.where(offset == slot - W, 1.0, 0.0).astype(F32), axis=1, keepdims=True)
        maskx[slot] = jnp.broadcast_to(hit, (NB, OBS))

    def lanes(place, count=1):
        return pl.ds(pl.multiple_of(place * OBS, OBS), count * OBS)

    def set_vectors(place, vectors):
        hi, lo = split(vectors)
        zx[0:16, lanes(place)] = hi
        zx[16:32, lanes(place)] = lo

    def set_left(place, members, crd):
        hi, lo = split(members)
        s1, s2, s3, base, x, y = position_parts(crd, place)
        one = jnp.ones((1, OBS), F32)
        parts = rows_of([s1, s2, s3, one, one, one, base, base, x, x, y])
        stacked = jnp.concatenate([hi, hi, lo, parts, jnp.zeros((48, OBS), BF16)], axis=0)
        lhsx[place - W] = stacked.T

    def set_right(place, members, crd):
        hi, lo = split(members * ENS_SCALE)
        s1, s2, s3, base, x, y = position_parts(crd, place)
        one = jnp.ones((1, OBS), F32)
        parts = rows_of([one, one, one, s1, s2, s3, -2.0 * base, -2.0 * x, -2.0 * base, -2.0 * x, -2.0 * y])
        rhs[place, 0:64, 0:128] = hi
        rhs[place, 64:128, 0:128] = lo
        rhs[place, 128:192, 0:128] = hi
        rhs[place, 192:256, 0:128] = jnp.zeros((64, OBS), BF16)
        rhs[place, 0:192, 128:256] = jnp.zeros((192, OBS), BF16)
        rhs[place, 192:208, 128:256] = parts
        rhs[place, 208:256, 128:256] = jnp.zeros((48, OBS), BF16)

    def prepare_own(i, carry):
        members = ens_v[i]
        vectors = v_v[i]
        set_left(i + W, members, crd_v[i])
        set_right(i + W, members, crd_v[i])
        set_vectors(i + W, vectors)
        zf[0:16, lanes(i)] = vectors
        zf[16:32, lanes(i)] = obs_v[pl.ds(i, 1), :] * vectors
        return carry

    lax.fori_loop(0, NB, prepare_own, 0)

    def tile(b, j, mask):
        both = jnp.dot(lhsx[b + j - W], rhs[b], preferred_element_type=F32)
        shared = both[:, 0:128]
        square = both[:, 128:256]
        inverse = lax.rsqrt(jnp.maximum(square, 1e-30))
        value = jnp.exp2(square * C_CORR * inverse) + jnp.exp2(square * C_LOC) * shared
        hi, lo = split(value * mask)
        kmat[b, j * OBS : (j + 1) * OBS, 0:128] = hi
        kmat[b, j * OBS : (j + 1) * OBS, 128:256] = lo

    def own_mask(b, j):
        return maskx[j + W, pl.ds(b - W, 1), :]

    def add(row, place, count, part):
        part = part[0:16] + part[16:32]
        zf[row : row + 16, lanes(place - W, count)] += part * STATIC_VAR

    def gather(b, start, stop, row):
        part = jnp.dot(
            zx[row : row + 32, lanes(b + start, stop - start)], kmat[b, start * OBS : stop * OBS, :],
            preferred_element_type=F32,
        )
        add(row // 2 + 16, b, 1, part[:, 0:128] + part[:, 128:256])

    def scatter(b, start, stop, row):
        vectors = zx[row : row + 32, lanes(b)]
        part = lax.dot_general(
            jnp.concatenate([vectors, vectors], axis=1), kmat[b, start * OBS : stop * OBS, :],
            (((1,), (1,)), ((), ())), preferred_element_type=F32,
        )
        add(row // 2 + 16, b + start, stop - start, part)

    last = NB

    def own_tiles(b, carry):
        for j in range(HALF):
            tile(b, j, own_mask(b, j))
        return carry

    def apply_own(b, row):
        gather(b, 0, HALF, row)
        scatter(b, 1, HALF, row)

    def first(b, carry):
        own_tiles(b, carry)
        apply_own(b, 0)
        return carry

    def second(b, carry):
        apply_own(b, 32)
        return carry

    def apply_last(row):
        for b in range(last, last + W):
            inside = last + W - b
            gather(b, 0, inside, row)
            if inside > 1:
                scatter(b, 1, inside, row)

    def apply_cross(row):
        for b in range(W):
            scatter(b, W - b, HALF, row)
            gather(last + b, W - b, HALF, row)

    lax.fori_loop(W, last, first, 0)
    for b in range(last, last + W):
        for j in range(last + W - b):
            tile(jnp.int32(b), j, own_mask(b, j))
    apply_last(0)
    for copy in static:
        copy.wait()

    def prepare_halo(i, carry):
        set_right(i, ens_lo[i], crd_lo[i])
        set_left(i + NB + W, ens_hi[i], crd_hi[i])
        set_vectors(i, v_lo[i])
        set_vectors(i + NB + W, v_hi[i])
        return carry

    lax.fori_loop(0, W, prepare_halo, 0)
    for b in range(W):
        for j in range(W - b, HALF):
            c = b + j
            tile(jnp.int32(b), j, maskx[W - j, c - W : c - W + 1, :])
            tile(jnp.int32(last + b), j, own_mask(last + b, j))
    apply_cross(0)

    moving = [
        remote(zf.at[16:32, (NB - W) * OBS : NB * OBS], p_lo, 6, right),
        remote(zf.at[16:32, 0 : W * OBS], p_hi, 7, left),
    ]
    for copy in moving:
        copy.start()

    def renew(row, source, start):
        hi, lo = split(source)
        zx[row : row + 16, start * OBS : start * OBS + source.shape[1]] = hi
        zx[row + 16 : row + 32, start * OBS : start * OBS + source.shape[1]] = lo

    product = zf[16:32, :]
    renew(32, product, W)

    def start_q(i, carry):
        zf[32:48, lanes(i)] = obs_v[pl.ds(i, 1), :] * zf[16:32, lanes(i)]
        return carry

    lax.fori_loop(0, NB, start_q, 0)
    lax.fori_loop(W, last, second, 0)
    apply_last(32)
    for copy in moving:
        copy.wait()
    renew(32, p_lo[...], 0)
    renew(32, p_hi[...], NB + W)
    apply_cross(32)
    renew(64, zf[32:48, :], W)

    inner = slice(W * OBS, (W + NB) * OBS)
    gram = lax.dot_general(
        zx[0:64, inner], zx[0:96, inner], (((1,), (1,)), ((), ())), preferred_element_type=F32
    )
    gram = jnp.concatenate([gram, jnp.zeros((64, 32), F32)], axis=1)
    lane = lax.broadcasted_iota(jnp.int32, (16, OBS), 1)
    lane8 = lax.broadcasted_iota(jnp.int32, (8, OBS), 1)

    def turn(value, by):
        return pltpu.roll(value, by % OBS, 1)

    of_r = gram[0:16] + gram[16:32]
    of_p = gram[32:48] + gram[48:64]
    of_r = of_r + turn(of_r, -16)
    of_p = of_p + turn(of_p, -16)
    even = (lane & 16) == 0
    own_part = jnp.where(even, of_r, turn(of_p, -16))
    part_a[...] = jnp.where(lane8 < 64, own_part[0:8], turn(own_part[8:16], 64))

    def exchange(part, red, peer, send, recv):
        def copy(step):
            return pltpu.make_async_remote_copy(
                src_ref=part, dst_ref=red.at[step - 1], send_sem=send.at[step - 1], recv_sem=recv.at[step - 1],
                device_id=peer(step), device_id_type=MESH,
            )

        def start(step, carry):
            copy(step).start()
            return carry

        def wait(step, carry):
            copy(step).wait()
            return carry

        lax.fori_loop(1, 16, start, 0)
        lax.fori_loop(1, 16, wait, 0)
        return part[...] + jnp.sum(red[...], axis=0)

    part_b[...] = exchange(part_a, red_a, peer_a, send_a, recv_a)
    packed = exchange(part_b, red_b, peer_b, send_b, recv_b)

    moments = jnp.concatenate([packed, turn(packed, 64)], axis=0)
    top = jnp.where(lane < 16, turn(moments, -32), jnp.where(lane < 32, moments, turn(moments, 32)))
    low = jnp.where(lane < 16, turn(moments, -16), jnp.where(lane < 32, turn(moments, -32), moments))
    system = jnp.concatenate([top, low], axis=0)
    rows = lax.broadcasted_iota(jnp.int32, (32, OBS), 0)
    for k in range(32):
        pivot = 1.0 / system[k : k + 1, k : k + 1]
        row = system[k : k + 1, :] * pivot
        system = jnp.where(rows == k, row, system - system[:, k : k + 1] * row)

    solved = jnp.concatenate([system, jnp.zeros((96, OBS), F32)], axis=0).T
    for_w = jnp.where(lane < 32, solved[32:48, :], 0.0)
    both = jnp.concatenate([for_w, turn(for_w, 16)], axis=0)[:, 0:48]
    for chunk in range(4):
        sums = jnp.dot(
            both, zf[:, chunk * 512 : (chunk + 1) * 512], preferred_element_type=F32, precision=lax.Precision.HIGHEST
        )
        for piece in range(4):
            b = chunk * 4 + piece
            here = sums[:, piece * OBS : (piece + 1) * OBS]
            out[b, 0:16, :] = here[0:16]
            out[b, 16:32, :] = zf[0:16, b * OBS : (b + 1) * OBS] - here[16:32]


def on_device(innovations, ensemble, coords, obs_error, pair_cols, pair_count):
    del pair_count
    out = pl.pallas_call(
        kernel,
        out_shape=jax.ShapeDtypeStruct((NB, 2 * RHS, OBS), F32),
        in_specs=[pl.BlockSpec(memory_space=pltpu.HBM)] * 5,
        out_specs=pl.BlockSpec(memory_space=pltpu.VMEM),
        scratch_shapes=[
            pltpu.VMEM((NB, MEM, OBS), F32),
            pltpu.VMEM((NB, 2, OBS), jnp.int32),
            pltpu.VMEM((NB, RHS, OBS), F32),
            pltpu.VMEM((NB, OBS), F32),
            pltpu.VMEM((NB, SLOTS), jnp.int32),
            pltpu.VMEM((NB + W, OBS, 256), BF16),
            pltpu.VMEM((NB + W, 256, 256), BF16),
            pltpu.VMEM((NB + W, HALF * OBS, 256), BF16),
            pltpu.VMEM((96, NX * OBS), BF16),
            pltpu.VMEM((48, NB * OBS), F32),
            pltpu.VMEM((SLOTS, NB, OBS), F32),
            pltpu.VMEM((W, MEM, OBS), F32),
            pltpu.VMEM((W, MEM, OBS), F32),
            pltpu.VMEM((W, 2, OBS), jnp.int32),
            pltpu.VMEM((W, 2, OBS), jnp.int32),
            pltpu.VMEM((W, RHS, OBS), F32),
            pltpu.VMEM((W, RHS, OBS), F32),
            pltpu.VMEM((RHS, W * OBS), F32),
            pltpu.VMEM((RHS, W * OBS), F32),
            pltpu.VMEM((8, OBS), F32),
            pltpu.VMEM((8, OBS), F32),
            pltpu.VMEM((15, 8, OBS), F32),
            pltpu.VMEM((15, 8, OBS), F32),
            pltpu.SemaphoreType.DMA((5,)),
            pltpu.SemaphoreType.DMA((8,)),
            pltpu.SemaphoreType.DMA((8,)),
            pltpu.SemaphoreType.DMA((15,)),
            pltpu.SemaphoreType.DMA((15,)),
            pltpu.SemaphoreType.DMA((15,)),
            pltpu.SemaphoreType.DMA((15,)),
        ],
        compiler_params=pltpu.CompilerParams(
            collective_id=0, has_side_effects=True, vmem_limit_bytes=56 * 1024 * 1024
        ),
    )(innovations, ensemble, coords, obs_error, pair_cols)
    return out[:, 0:RHS], out[:, RHS:]


def solution(mesh):
    both = ("region", "sub")
    in_specs = (
        P(both, None, None),
        P(both, None, None),
        P(both, None, None),
        P(both, None),
        P(both, None),
        P(both),
    )
    out_specs = (P(both, None, None), P(both, None, None))
    return jax.shard_map(on_device, mesh=mesh, in_specs=in_specs, out_specs=out_specs, check_vma=False)
```

time: 48.6 us -> 43 us (0.88)
  local copies, waits for them, and re-layouts: 5.36 us -> 1.69 us
  Pallas kernels: 42.3 us -> 40.5 us
    unnamed x12 -> x0, local copies, waits for them, and re-layouts: 5.36 us -> none
    pallas_call x1, Pallas kernels: 42.3 us -> 40.5 us  [on_device(): pl.pallas_call(kernel, out_shape=jax.ShapeDtypeStruct((NB, 2 * RHS, OBS),...]
    slice x0 -> x1, local copies, waits for them, and re-layouts: none -> 1.69 us  [on_device(): return (out[:, 0:RHS], out[:, RHS:])]
where the time goes in v1:
time: 43 us; the launch traced here: 42.9 us
  Pallas kernels  40.5 us (94%)
  local copies, waits for them, and re-layouts  1.69 us (4%)
  between operations  0.64 us (1%)
    pallas_call x1, Pallas kernels, on_device(): pl.pallas_call(kernel, out_shape=jax.ShapeDtypeStruct((NB, 2 * RHS, OBS),...  40.5 us
    slice x1, local copies, waits for them, and re-layouts, on_device(): return (out[:, 0:RHS], out[:, RHS:])  1.69 us

profile of v1, /device:TPU:1, one launch (start us, length us, event | category | flops | bytes accessed | tf_op | source)
XLA Modules:
  0.0 42.9 jit_solution(14083714285354665798)
XLA Ops:
  0.6 40.5 %shard_map.68 = f32[16,32,128]{2,1,0:T(8,128)} custom-call(f32[16,16,128]{2,1,0:T(8,128)} %innov.1, f32[16,64,128]{2,1,0:T(8,128)} %ens.1, s32[16,2,128]{2,1,0:T(2,128)} %coords.1, f32[16,128]{1,0:T(8,128)} %obs.1, s32[16,9]{1,0:T(8,128)} %cols.1), custom_call_target="tpu_custom_call" | custom-call | tf_op jit(solution)/shard_map/pallas_call | solution.py:350
  41.2 1.7 %fusion = (f32[16,16,128]{2,1,0:T(8,128)}, f32[16,16,128]{2,1,0:T(8,128)}) fusion(f32[16,32,128]{2,1,0:T(8,128)} %shard_map.68), kind=kLoop, calls=%fused_computation | loop fusion | bytes 524288 | tf_op jit(solution)/shard_map/slice | solution.py:391
